TPU v7x, 128 devices: a whole 4x4x4 slice. The times are simulated.
128 devices in a mesh: dp: 8 (over z, x_lo), seq: 16 (over y, x_hi, core).
Axes of the slice: x: 4 (x_hi: 2, x_lo: 2; x = x_hi * 2 + x_lo), y: 4, z: 4, core: 2. Of those that a mesh axis runs over, the one named last changes fastest.
Arguments:
- frames: bfloat16 [8, 4096, 1536], P('dp', 'seq'), may hold values from -6 to 6
- upstream: bfloat16 [8, 4096, 1536], P('dp', 'seq'), may hold values from -6 to 6
- utt_span: int32 [2, 8, 4096], P(None, 'dp', 'seq'), may hold values from 0 to 4096, as said below
- w_qkv: bfloat16 [1536, 2304], P('dp')
- w_out: bfloat16 [768, 1536], P('dp'), may hold values from -0.21875 to 0.21875
Outputs:
- branch: bfloat16 [8, 4096, 1536], P('dp', 'seq')
- grad_in: bfloat16 [8, 4096, 1536], P('dp', 'seq')
- grad_qkv: float32 [1536, 2304], P(('dp', 'seq'))
- grad_out: float32 [768, 1536], P(('dp', 'seq'))
Inputs may be any that keep to these rules, and one draw needn't show every extreme that they name: In each row the utterances tile the frames: for frame i, utt_span[0] <= i < utt_span[1], and all frames of an utterance carry the same pair.
All inputs are finite; a program needn't handle non-finite values.
Results may differ from a plain program's by a relative error of at most 0.015.
Values may be sent and summed in bfloat16 or wider, within the bound.
No kernel may reach another device: no remote copies, remote signals or barrier semaphores. Data moves between devices by JAX's collectives and lax.ppermute only.
A program may use at most 128 MiB of HBM per device.

v0:
```python
import jax
import jax.numpy as jnp
from jax import lax
from jax.sharding import PartitionSpec as P

HEADS = 12
HEAD_DIM = 64
STRETCH = 64
PRIOR = 4
EPS = 1e-05


def from_behind(value, axis, by):
    length = lax.axis_size(axis)
    pairs = [(i, i + by) for i in range(length) if 0 <= i + by < length]
    return lax.ppermute(value, axis, pairs)


def normalize(inputs):
    widened = inputs.astype(jnp.float32)
    centered = widened - jnp.mean(widened, axis=-1, keepdims=True)
    inv_sigma = lax.rsqrt(jnp.mean(centered * centered, axis=-1, keepdims=True) + EPS)
    return (centered * inv_sigma, inv_sigma)


def contract(form, left, right):
    return jnp.einsum(form, left, right, preferred_element_type=jnp.float32)


def windows(extended):
    stretch_total = extended.shape[0] // STRETCH
    stretch_count = stretch_total - PRIOR
    blocked = extended.reshape((stretch_total, STRETCH) + extended.shape[1:])
    return jnp.concatenate(
        [blocked[shift_by : shift_by + stretch_count] for shift_by in range(PRIOR + 1)], axis=1
    )


def unwindow(windowed):
    stretch_count = windowed.shape[0]
    parted = windowed.reshape((stretch_count, PRIOR + 1, STRETCH) + windowed.shape[2:])
    running = jnp.zeros((stretch_count + PRIOR, STRETCH) + windowed.shape[2:], jnp.float32)
    for shift_by in range(PRIOR + 1):
        running = running.at[shift_by : shift_by + stretch_count].add(parted[:, shift_by])
    return running.reshape(((stretch_count + PRIOR) * STRETCH,) + windowed.shape[2:])


def visible(starts, limits, offset):
    stretch_count = starts.shape[0] // STRETCH
    block_first = jnp.arange(stretch_count, dtype=jnp.int32)[:, None] * STRETCH
    key_pos = (
        offset
        - PRIOR * STRETCH
        + block_first
        + jnp.arange((PRIOR + 1) * STRETCH, dtype=jnp.int32)[None, :]
    )
    lowest = starts.reshape(stretch_count, STRETCH)
    beyond = limits.reshape(stretch_count, STRETCH)
    return (key_pos[:, None, :] >= lowest[:, :, None]) & (key_pos[:, None, :] < beyond[:, :, None])


def attend_forward(queries, keys_ext, values_ext, mask):
    stretch_count = queries.shape[0] // STRETCH
    query_blocks = queries.reshape(stretch_count, STRETCH, HEADS, HEAD_DIM)
    key_windows = windows(keys_ext.reshape(-1, HEADS, HEAD_DIM))
    value_windows = windows(values_ext.reshape(-1, HEADS, HEAD_DIM))
    scores = contract("nqhd,nkhd->nhqk", query_blocks, key_windows) * HEAD_DIM ** (-0.5)
    allowed = mask[:, None]
    masked = jnp.where(allowed, scores, -1e30)
    highest = jnp.max(masked, axis=-1, keepdims=True)
    weights = jnp.where(allowed, jnp.exp(masked - highest), 0.0)
    probs = weights / jnp.sum(weights, axis=-1, keepdims=True)
    probs_low = probs.astype(jnp.bfloat16)
    context = contract("nhqk,nkhd->nqhd", probs_low, value_windows).astype(jnp.bfloat16)
    return (
        context.reshape(queries.shape),
        (query_blocks, key_windows, value_windows, probs, probs_low),
    )


def attend_backward(saved, d_context):
    query_blocks, key_windows, value_windows, probs, probs_low = saved
    d_blocks = d_context.reshape(query_blocks.shape)
    d_probs = contract("nqhd,nkhd->nhqk", d_blocks, value_windows)
    d_scores = probs * (d_probs - jnp.sum(probs * d_probs, axis=-1, keepdims=True))
    d_scores_low = (d_scores * HEAD_DIM ** (-0.5)).astype(jnp.bfloat16)
    d_queries = contract("nhqk,nkhd->nqhd", d_scores_low, key_windows).astype(jnp.bfloat16)
    d_keys = unwindow(contract("nhqk,nqhd->nkhd", d_scores_low, query_blocks))
    d_values = unwindow(contract("nhqk,nqhd->nkhd", probs_low, d_blocks))
    ext_rows = d_keys.shape[0]
    return (
        d_queries.reshape(d_context.shape),
        d_keys.reshape(ext_rows, -1),
        d_values.reshape(ext_rows, -1),
    )


def against_rows(left, piece_rows):
    return lax.dot_general(
        left, piece_rows, (((1,), (1,)), ((), ())), preferred_element_type=jnp.float32
    )


def over_frames(left, right):
    return lax.dot_general(
        left, right, (((0,), (0,)), ((), ())), preferred_element_type=jnp.float32
    )


def joint_term(left, right):
    return over_frames(left, right)


def body(frames, upstream, utt_span, w_qkv, w_out):
    own_frames = frames[0]
    own_grad = upstream[0]
    frame_count = own_frames.shape[0]
    inner_width = w_qkv.shape[1] // 3
    halo_rows = PRIOR * STRETCH
    offset = lax.axis_index("seq") * frame_count
    normed, inv_sigma = normalize(own_frames)
    normed_low = normed.astype(jnp.bfloat16)
    full_qkv, full_out = (
        lax.all_gather(w_qkv, "dp", axis=0, tiled=True),
        lax.all_gather(w_out, "dp", axis=0, tiled=True),
    )
    projected = jnp.dot(normed_low, full_qkv, preferred_element_type=jnp.float32)
    projected = projected.astype(jnp.bfloat16)
    queries = projected[:, :inner_width]
    keys_all = projected[:, inner_width : 2 * inner_width]
    values_all = projected[:, 2 * inner_width :]
    history = from_behind(jnp.stack([keys_all, values_all]), "seq", 1)
    keys_ext = jnp.concatenate([history[0], keys_all], axis=0)
    values_ext = jnp.concatenate([history[1], values_all], axis=0)
    context, saved = attend_forward(
        queries, keys_ext, values_ext, visible(utt_span[0, 0], utt_span[1, 0], offset)
    )
    branch = jnp.dot(context, full_out, preferred_element_type=jnp.float32)
    d_context = against_rows(own_grad, full_out)
    branch = branch.astype(jnp.bfloat16)
    d_context = d_context.astype(jnp.bfloat16)
    d_queries, d_keys, d_values = attend_backward(saved, d_context)
    returned = from_behind(
        jnp.stack([d_keys[:halo_rows], d_values[:halo_rows]]).astype(jnp.bfloat16), "seq", -1
    ).astype(jnp.float32)
    d_keys_own = (
        d_keys[halo_rows:].at[frame_count - halo_rows :].add(returned[0]).astype(jnp.bfloat16)
    )
    d_values_own = (
        d_values[halo_rows:].at[frame_count - halo_rows :].add(returned[1]).astype(jnp.bfloat16)
    )
    d_proj = jnp.concatenate([d_queries, d_keys_own, d_values_own], axis=1)
    grad_qkv = lax.psum_scatter(
        joint_term(normed_low, d_proj), ("dp", "seq"), scatter_dimension=0, tiled=True
    )
    grad_out = lax.psum_scatter(
        joint_term(context, own_grad), ("dp", "seq"), scatter_dimension=0, tiled=True
    )
    d_normed = against_rows(d_proj, full_qkv)
    grad_in = inv_sigma * (
        d_normed
        - jnp.mean(d_normed, axis=-1, keepdims=True)
        - normed * jnp.mean(d_normed * normed, axis=-1, keepdims=True)
    )
    return (branch[None], grad_in.astype(jnp.bfloat16)[None], grad_qkv, grad_out)


def solution(mesh):
    in_specs = (
        P("dp", "seq", None),
        P("dp", "seq", None),
        P(None, "dp", "seq"),
        P("dp", None),
        P("dp", None),
    )
    out_specs = (
        P("dp", "seq", None),
        P("dp", "seq", None),
        P(("dp", "seq"), None),
        P(("dp", "seq"), None),
    )
    return jax.shard_map(body, mesh=mesh, in_specs=in_specs, out_specs=out_specs, check_vma=False)
```

profile of v0, /device:TPU:8, one launch (start us, length us, event | category | flops | bytes accessed | tf_op | source)
XLA Modules:
  0.0 1096.6 jit_solution(9958152777341482748)
XLA Ops:
  11.1 144.9 %all-gather.3.cloned.1.call-done = bf16[1536,2304]{1,0:T(8,128)(2,1)} async-done(((bf16[192,2304]{1,0:T(8,128)(2,1)}), bf16[1536,2304]{1,0:T(8,128)(2,1)}) %all-gather.3.cloned.1.call-update) | async-done | bytes 7077904 | tf_op jit(solution)/shard_map/all_gather | solution.py:124
  156.0 5.1 convolution_convert_fusion
  164.6 58.0 %all-gather.5.cloned.1.call-done = bf16[768,1536]{1,0:T(8,128)(2,1)} async-done(((bf16[96,1536]{1,0:T(8,128)(2,1)}), bf16[768,1536]{1,0:T(8,128)(2,1)}) %all-gather.5.cloned.1.call-update) | async-done | bytes 2359312 | tf_op jit(solution)/shard_map/all_gather | solution.py:125
  257.2 4.6 concatenate.42
  261.8 4.2 fusion.87
  266.0 5.8 concatenate.44
  271.9 6.3 fusion.86
  278.1 4.4 fusion.51
  282.5 2.8 convolution_bitcast_fusion
  285.3 6.9 copy.108
  299.0 24.8 %fusion.20 = f32[4,320,12,64]{1,3,2,0:T(8,128)} fusion(bf16[4,64,12,64]{1,3,2,0:T(8,128)(2,1)S(1)} %copy-done.19, f32[4,12,64,320]{3,2,1,0:T(8,128)} %fusion.87, f32[4,12,64,320]{3,2,1,0:T(8,128)} %get-tuple-element.190, f32[4,12,64]{2,1,0:T(8,128)S(1)} %get-tuple-element.189), kind=kOutput, calls=%fused_computation.20 | convolution fusion | flops 132713792 | bytes 12201984 | tf_op jit(solution)/shard_map/nhqk,nqhd->nkhd/dot_general | solution.py:27
  324.9 6.9 copy.100
  341.1 4.3 collective-permute-start.1
  345.4 24.3 %fusion.52 = bf16[4,64,12,64]{1,3,2,0:T(8,128)(2,1)S(1)} fusion(bf16[4,320,12,64]{1,3,2,0:T(8,128)(2,1)} %concatenate.44, f32[4,12,64,320]{3,2,1,0:T(8,128)} %fusion.87, f32[4,12,64,320]{3,2,1,0:T(8,128)} %get-tuple-element.190, f32[4,12,64]{2,1,0:T(8,128)} %copy-done.78), kind=kOutput, calls=%fused_computation.63 | convolution fusion | flops 132910400 | bytes 10235904 | tf_op jit(solution)/shard_map/nhqk,nkhd->nqhd/dot_general | solution.py:27
  375.8 3.4 fusion.41
  382.8 3.0 fusion.62
  388.5 7.3 fusion.65
  395.8 379.2 %fusion.84 = (f32[16,2304]{1,0:T(8,128)S(1)}, f32[8,1536]{1,0:T(8,128)S(1)}) fusion(f32[1536,2304]{1,0:T(8,128)} %fusion.65, f32[768,1536]{1,0:T(8,128)} %fusion.62), kind=kCustom, calls=%all-reduce-scatter.2 | all-reduce-scatter fusion | flops 6291458 | bytes 19070976
  779.1 11.9 %collective-permute-start.62 = (f32[8,1536]{1,0:T(8,128)S(1)}, f32[8,1536]{1,0:T(8,128)S(1)}, u32[]{:S(2)}, u32[]{:S(2)}) collective-permute-start(f32[8,1536]{1,0:T(8,128)S(1)} %get-tuple-element.171), channel_id=1, source_target_pairs={{0,29},{1,30},{2,31},{3,32},{4,33},{5,34},{6,35},{7,36},{8,37},{9,... | collective-permute-start | bytes 147464
  799.2 15.5 %collective-permute-start.55 = (f32[8,1536]{1,0:T(8,128)S(1)}, f32[8,1536]{1,0:T(8,128)S(1)}, u32[]{:S(2)}, u32[]{:S(2)}) collective-permute-start(f32[8,1536]{1,0:T(8,128)S(1)} %get-tuple-element.171), channel_id=1, source_target_pairs={{0,22},{1,23},{2,24},{3,25},{4,26},{5,27},{6,28},{7,29},{8,30},{9,... | collective-permute-start | bytes 147464
  816.0 2.6 collective-permute-start.53
  818.6 2.9 collective-permute-start.52
  826.3 3.1 collective-permute-start.48
  831.9 3.5 collective-permute-start.46
  840.1 5.1 collective-permute-start.43
  848.9 5.8 collective-permute-start.40
  859.3 2.5 collective-permute-start.39
  863.8 2.8 collective-permute-start.37
  866.6 6.1 collective-permute-start.36
  872.7 3.1 collective-permute-start.35
  886.4 3.1 collective-permute-start.27
  889.5 3.3 fusion.14
  897.6 11.2 %collective-permute-done.29 = f32[16,2304]{1,0:T(8,128)S(1)} collective-permute-done((f32[16,2304]{1,0:T(8,128)S(1)}, f32[16,2304]{1,0:T(8,128)S(1)}, u32[]{:S(2)}, u32[]{:S(2)}) %collective-permute-start.29) | collective-permute-done | bytes 147488
  910.1 3.2 collective-permute-start.23
  915.5 5.3 fusion.83
  922.1 4.6 collective-permute-start.20
  932.4 4.3 collective-permute-start.16
  938.4 4.3 collective-permute-start.14
  942.8 5.7 collective-permute-start.13
  949.9 9.1 collective-permute-start.11
  960.9 5.9 collective-permute-start.9
  969.1 2.5 collective-permute-start.7
  973.1 28.8 %concatenate.47 = f32[262,1536]{1,0:T(8,128)S(1)} concatenate(f32[6,1536]{1,0:T(8,128)} %copy-done.49, f32[8,1536]{1,0:T(8,128)S(1)} %collective-permute-done.64, f32[8,1536]{1,0:T(8,128)} %copy-done.50, f32[8,1536]{1,0:T(8,128)} %copy-done.51, f32[8,1536]{1,0:T(8,128)} %copy-done.52, f32[8,1536]{1,0:T(8,128)} %copy-done.53, f32[8,1536]{1,0:T(8,128)} %copy-done.54, ...), dimensions={0} | concatenate | bytes 3219456
  1001.9 10.0 collective-permute-start.6
  1014.1 2.5 collective-permute-start.4
  1016.6 6.3 collective-permute-start.3
  1025.6 2.8 collective-permute-done.4
  1032.0 56.0 %concatenate.46 = f32[524,2304]{1,0:T(8,128)} concatenate(f32[12,2304]{1,0:T(8,128)} %collective-permute-done.33, f32[16,2304]{1,0:T(8,128)} %collective-permute-done.32, f32[16,2304]{1,0:T(8,128)S(1)} %copy-done.22, f32[16,2304]{1,0:T(8,128)S(1)} %copy-done.24, f32[16,2304]{1,0:T(8,128)S(1)} %copy-done.26, f32[16,2304]{1,0:T(8,128)S(1)} %collective-permute-done.28, ...), dimensions={0} | concatenate | bytes 9658368
  (341 shorter events, 150.2 us)
Async XLA Ops:
  7.2 148.8 %all-gather.3.cloned.1.call-start = ((), (), s32[]{:S(2)}) async-start(), calls=%async_computation | async-start | bytes 7962624 | tf_op jit(solution)/shard_map/all_gather | solution.py:124
  7.9 214.6 %all-gather.5.cloned.1.call-start = ((), (), s32[]{:S(2)}) async-start(), calls=%async_computation.1 | async-start | bytes 2654208 | tf_op jit(solution)/shard_map/all_gather | solution.py:125
  162.2 72.0 %collective-permute-start = (bf16[2,256,768]{2,1,0:T(8,128)(2,1)}, bf16[2,256,768]{2,1,0:T(8,128)(2,1)}, u32[]{:S(2)}, u32[]{:S(2)}) collective-permute-start(bf16[2,256,768]{2,1,0:T(8,128)(2,1)} %pad_maximum_fusion.1), channel_id=1, source_target_pairs={{0,1},{1,2},{2,3},{3,4},{4,5},{5,6},{6,7},{7,8},{8,9},{9,10},{10,1... | collective-permute-start | bytes 2359304 | tf_op jit(solution)/shard_map/ppermute | solution.py:16
  341.1 44.7 %collective-permute-start.1 = (bf16[2,256,768]{1,2,0:T(8,128)(2,1)}, bf16[2,256,768]{1,2,0:T(8,128)(2,1)}, u32[]{:S(2)}, u32[]{:S(2)}) collective-permute-start(bf16[2,256,768]{1,2,0:T(8,128)(2,1)} %pad_maximum_fusion.2), channel_id=1, source_target_pairs={{1,0},{2,1},{3,2},{4,3},{5,4},{6,5},{7,6},{8,7},{9,8},{10,9},{11,1... | collective-permute-start | bytes 2359304 | tf_op jit(solution)/shard_map/ppermute | solution.py:16
  775.0 18.8 %collective-permute-start.64 = (f32[8,1536]{1,0:T(8,128)S(1)}, f32[8,1536]{1,0:T(8,128)S(1)}, u32[]{:S(2)}, u32[]{:S(2)}) collective-permute-start(f32[8,1536]{1,0:T(8,128)S(1)} %get-tuple-element.171), channel_id=1, source_target_pairs={{0,31},{1,32},{2,33},{3,34},{4,35},{5,36},{6,37},{7,38},{8,39},{9,... | collective-permute-start | bytes 147464
  776.5 16.1 %collective-permute-start.65 = (f32[6,1536]{1,0:T(8,128)S(1)}, f32[6,1536]{1,0:T(8,128)S(1)}, u32[]{:S(2)}, u32[]{:S(2)}) collective-permute-start(f32[6,1536]{1,0:T(8,128)S(1)} %slice.520), channel_id=1, source_target_pairs={{0,32},{1,33},{2,34},{3,35},{4,36},{5,37},{6,38},{7,39},{8,40},{9,... | collective-permute-start | bytes 110600
  777.8 17.4 %collective-permute-start.63 = (f32[8,1536]{1,0:T(8,128)S(1)}, f32[8,1536]{1,0:T(8,128)S(1)}, u32[]{:S(2)}, u32[]{:S(2)}) collective-permute-start(f32[8,1536]{1,0:T(8,128)S(1)} %get-tuple-element.171), channel_id=1, source_target_pairs={{0,30},{1,31},{2,32},{3,33},{4,34},{5,35},{6,36},{7,37},{8,38},{9,... | collective-permute-start | bytes 147464
  779.1 17.4 %collective-permute-start.62 = (f32[8,1536]{1,0:T(8,128)S(1)}, f32[8,1536]{1,0:T(8,128)S(1)}, u32[]{:S(2)}, u32[]{:S(2)}) collective-permute-start(f32[8,1536]{1,0:T(8,128)S(1)} %get-tuple-element.171), channel_id=1, source_target_pairs={{0,29},{1,30},{2,31},{3,32},{4,33},{5,34},{6,35},{7,36},{8,37},{9,... | collective-permute-start | bytes 147464
  793.9 20.7 %collective-permute-start.59 = (f32[8,1536]{1,0:T(8,128)S(1)}, f32[8,1536]{1,0:T(8,128)S(1)}, u32[]{:S(2)}, u32[]{:S(2)}) collective-permute-start(f32[8,1536]{1,0:T(8,128)S(1)} %get-tuple-element.171), channel_id=1, source_target_pairs={{0,26},{1,27},{2,28},{3,29},{4,30},{5,31},{6,32},{7,33},{8,34},{9,... | collective-permute-start | bytes 147464
  795.2 20.7 %collective-permute-start.58 = (f32[8,1536]{1,0:T(8,128)S(1)}, f32[8,1536]{1,0:T(8,128)S(1)}, u32[]{:S(2)}, u32[]{:S(2)}) collective-permute-start(f32[8,1536]{1,0:T(8,128)S(1)} %get-tuple-element.171), channel_id=1, source_target_pairs={{0,25},{1,26},{2,27},{3,28},{4,29},{5,30},{6,31},{7,32},{8,33},{9,... | collective-permute-start | bytes 147464
  796.5 22.0 %collective-permute-start.57 = (f32[8,1536]{1,0:T(8,128)S(1)}, f32[8,1536]{1,0:T(8,128)S(1)}, u32[]{:S(2)}, u32[]{:S(2)}) collective-permute-start(f32[8,1536]{1,0:T(8,128)S(1)} %get-tuple-element.171), channel_id=1, source_target_pairs={{0,24},{1,25},{2,26},{3,27},{4,28},{5,29},{6,30},{7,31},{8,32},{9,... | collective-permute-start | bytes 147464
  797.8 23.6 %collective-permute-start.56 = (f32[8,1536]{1,0:T(8,128)S(1)}, f32[8,1536]{1,0:T(8,128)S(1)}, u32[]{:S(2)}, u32[]{:S(2)}) collective-permute-start(f32[8,1536]{1,0:T(8,128)S(1)} %get-tuple-element.171), channel_id=1, source_target_pairs={{0,23},{1,24},{2,25},{3,26},{4,27},{5,28},{6,29},{7,30},{8,31},{9,... | collective-permute-start | bytes 147464
  799.2 24.5 %collective-permute-start.55 = (f32[8,1536]{1,0:T(8,128)S(1)}, f32[8,1536]{1,0:T(8,128)S(1)}, u32[]{:S(2)}, u32[]{:S(2)}) collective-permute-start(f32[8,1536]{1,0:T(8,128)S(1)} %get-tuple-element.171), channel_id=1, source_target_pairs={{0,22},{1,23},{2,24},{3,25},{4,26},{5,27},{6,28},{7,29},{8,30},{9,... | collective-permute-start | bytes 147464
  826.3 13.8 %collective-permute-start.48 = (f32[8,1536]{1,0:T(8,128)S(1)}, f32[8,1536]{1,0:T(8,128)S(1)}, u32[]{:S(2)}, u32[]{:S(2)}) collective-permute-start(f32[8,1536]{1,0:T(8,128)S(1)} %get-tuple-element.171), channel_id=1, source_target_pairs={{0,15},{1,16},{2,17},{3,18},{4,19},{5,20},{6,21},{7,22},{8,23},{9,... | collective-permute-start | bytes 147464
  829.5 15.8 %collective-permute-start.47 = (f32[8,1536]{1,0:T(8,128)S(1)}, f32[8,1536]{1,0:T(8,128)S(1)}, u32[]{:S(2)}, u32[]{:S(2)}) collective-permute-start(f32[8,1536]{1,0:T(8,128)S(1)} %get-tuple-element.171), channel_id=1, source_target_pairs={{0,14},{1,15},{2,16},{3,17},{4,18},{5,19},{6,20},{7,21},{8,22},{9,... | collective-permute-start | bytes 147464
  831.9 14.7 %collective-permute-start.46 = (f32[8,1536]{1,0:T(8,128)S(1)}, f32[8,1536]{1,0:T(8,128)S(1)}, u32[]{:S(2)}, u32[]{:S(2)}) collective-permute-start(f32[8,1536]{1,0:T(8,128)S(1)} %get-tuple-element.171), channel_id=1, source_target_pairs={{0,13},{1,14},{2,15},{3,16},{4,17},{5,18},{6,19},{7,20},{8,21},{9,... | collective-permute-start | bytes 147464
  837.7 17.0 %collective-permute-start.44 = (f32[8,1536]{1,0:T(8,128)S(1)}, f32[8,1536]{1,0:T(8,128)S(1)}, u32[]{:S(2)}, u32[]{:S(2)}) collective-permute-start(f32[8,1536]{1,0:T(8,128)S(1)} %get-tuple-element.171), channel_id=1, source_target_pairs={{0,11},{1,12},{2,13},{3,14},{4,15},{5,16},{6,17},{7,18},{8,19},{9,... | collective-permute-start | bytes 147464
  840.1 17.1 %collective-permute-start.43 = (f32[8,1536]{1,0:T(8,128)S(1)}, f32[8,1536]{1,0:T(8,128)S(1)}, u32[]{:S(2)}, u32[]{:S(2)}) collective-permute-start(f32[8,1536]{1,0:T(8,128)S(1)} %get-tuple-element.171), channel_id=1, source_target_pairs={{0,10},{1,11},{2,12},{3,13},{4,14},{5,15},{6,16},{7,17},{8,18},{9,... | collective-permute-start | bytes 147464
  845.3 13.9 %collective-permute-start.42 = (f32[8,1536]{1,0:T(8,128)S(1)}, f32[8,1536]{1,0:T(8,128)S(1)}, u32[]{:S(2)}, u32[]{:S(2)}) collective-permute-start(f32[8,1536]{1,0:T(8,128)S(1)} %get-tuple-element.171), channel_id=1, source_target_pairs={{0,9},{1,10},{2,11},{3,12},{4,13},{5,14},{6,15},{7,16},{8,17},{9,1... | collective-permute-start | bytes 147464
  846.6 15.2 %collective-permute-start.41 = (f32[8,1536]{1,0:T(8,128)S(1)}, f32[8,1536]{1,0:T(8,128)S(1)}, u32[]{:S(2)}, u32[]{:S(2)}) collective-permute-start(f32[8,1536]{1,0:T(8,128)S(1)} %get-tuple-element.171), channel_id=1, source_target_pairs={{0,8},{1,9},{2,10},{3,11},{4,12},{5,13},{6,14},{7,15},{8,16},{9,17... | collective-permute-start | bytes 147464
  848.9 14.8 %collective-permute-start.40 = (f32[8,1536]{1,0:T(8,128)S(1)}, f32[8,1536]{1,0:T(8,128)S(1)}, u32[]{:S(2)}, u32[]{:S(2)}) collective-permute-start(f32[8,1536]{1,0:T(8,128)S(1)} %get-tuple-element.171), channel_id=1, source_target_pairs={{0,7},{1,8},{2,9},{3,10},{4,11},{5,12},{6,13},{7,14},{8,15},{9,16}... | collective-permute-start | bytes 147464
  855.3 31.1 %collective-permute-start.32 = (f32[16,2304]{1,0:T(8,128)S(1)}, f32[16,2304]{1,0:T(8,128)}, u32[]{:S(2)}, u32[]{:S(2)}) collective-permute-start(f32[16,2304]{1,0:T(8,128)S(1)} %get-tuple-element.170), channel_id=1, source_target_pairs={{0,31},{1,32},{2,33},{3,34},{4,35},{5,36},{6,37},{7,38},{8,39},{9,... | collective-permute-start | bytes 442376
  857.3 27.7 %collective-permute-start.33 = (f32[12,2304]{1,0:T(8,128)S(1)}, f32[12,2304]{1,0:T(8,128)}, u32[]{:S(2)}, u32[]{:S(2)}) collective-permute-start(f32[12,2304]{1,0:T(8,128)S(1)} %slice.519), channel_id=1, source_target_pairs={{0,32},{1,33},{2,34},{3,35},{4,36},{5,37},{6,38},{7,39},{8,40},{9,... | collective-permute-start | bytes 331784
  877.8 15.0 %collective-permute-start.31 = (f32[16,2304]{1,0:T(8,128)S(1)}, f32[16,2304]{1,0:T(8,128)S(1)}, u32[]{:S(2)}, u32[]{:S(2)}) collective-permute-start(f32[16,2304]{1,0:T(8,128)S(1)} %get-tuple-element.170), channel_id=1, source_target_pairs={{0,30},{1,31},{2,32},{3,33},{4,34},{5,35},{6,36},{7,37},{8,38},{9,... | collective-permute-start | bytes 442376
  881.2 15.1 %collective-permute-start.30 = (f32[16,2304]{1,0:T(8,128)S(1)}, f32[16,2304]{1,0:T(8,128)S(1)}, u32[]{:S(2)}, u32[]{:S(2)}) collective-permute-start(f32[16,2304]{1,0:T(8,128)S(1)} %get-tuple-element.170), channel_id=1, source_target_pairs={{0,29},{1,30},{2,31},{3,32},{4,33},{5,34},{6,35},{7,36},{8,37},{9,... | collective-permute-start | bytes 442376
  883.7 25.0 %collective-permute-start.29 = (f32[16,2304]{1,0:T(8,128)S(1)}, f32[16,2304]{1,0:T(8,128)S(1)}, u32[]{:S(2)}, u32[]{:S(2)}) collective-permute-start(f32[16,2304]{1,0:T(8,128)S(1)} %get-tuple-element.170), channel_id=1, source_target_pairs={{0,28},{1,29},{2,30},{3,31},{4,32},{5,33},{6,34},{7,35},{8,36},{9,... | collective-permute-start | bytes 442376
  885.0 25.0 %collective-permute-start.28 = (f32[16,2304]{1,0:T(8,128)S(1)}, f32[16,2304]{1,0:T(8,128)S(1)}, u32[]{:S(2)}, u32[]{:S(2)}) collective-permute-start(f32[16,2304]{1,0:T(8,128)S(1)} %get-tuple-element.170), channel_id=1, source_target_pairs={{0,27},{1,28},{2,29},{3,30},{4,31},{5,32},{6,33},{7,34},{8,35},{9,... | collective-permute-start | bytes 442376
  886.4 26.9 %collective-permute-start.27 = (f32[16,2304]{1,0:T(8,128)S(1)}, f32[16,2304]{1,0:T(8,128)S(1)}, u32[]{:S(2)}, u32[]{:S(2)}) collective-permute-start(f32[16,2304]{1,0:T(8,128)S(1)} %get-tuple-element.170), channel_id=1, source_target_pairs={{0,26},{1,27},{2,28},{3,29},{4,30},{5,31},{6,32},{7,33},{8,34},{9,... | collective-permute-start | bytes 442376
  892.9 27.9 %collective-permute-start.26 = (f32[16,2304]{1,0:T(8,128)S(1)}, f32[16,2304]{1,0:T(8,128)S(1)}, u32[]{:S(2)}, u32[]{:S(2)}) collective-permute-start(f32[16,2304]{1,0:T(8,128)S(1)} %get-tuple-element.170), channel_id=1, source_target_pairs={{0,25},{1,26},{2,27},{3,28},{4,29},{5,30},{6,31},{7,32},{8,33},{9,... | collective-permute-start | bytes 442376
  896.3 25.8 %collective-permute-start.25 = (f32[16,2304]{1,0:T(8,128)S(1)}, f32[16,2304]{1,0:T(8,128)S(1)}, u32[]{:S(2)}, u32[]{:S(2)}) collective-permute-start(f32[16,2304]{1,0:T(8,128)S(1)} %get-tuple-element.170), channel_id=1, source_target_pairs={{0,24},{1,25},{2,26},{3,27},{4,28},{5,29},{6,30},{7,31},{8,32},{9,... | collective-permute-start | bytes 442376
  908.8 17.9 %collective-permute-start.24 = (f32[16,2304]{1,0:T(8,128)S(1)}, f32[16,2304]{1,0:T(8,128)S(1)}, u32[]{:S(2)}, u32[]{:S(2)}) collective-permute-start(f32[16,2304]{1,0:T(8,128)S(1)} %get-tuple-element.170), channel_id=1, source_target_pairs={{0,23},{1,24},{2,25},{3,26},{4,27},{5,28},{6,29},{7,30},{8,31},{9,... | collective-permute-start | bytes 442376
  910.1 19.1 %collective-permute-start.23 = (f32[16,2304]{1,0:T(8,128)S(1)}, f32[16,2304]{1,0:T(8,128)S(1)}, u32[]{:S(2)}, u32[]{:S(2)}) collective-permute-start(f32[16,2304]{1,0:T(8,128)S(1)} %get-tuple-element.170), channel_id=1, source_target_pairs={{0,22},{1,23},{2,24},{3,25},{4,26},{5,27},{6,28},{7,29},{8,30},{9,... | collective-permute-start | bytes 442376
  914.0 16.6 %collective-permute-start.22 = (f32[16,2304]{1,0:T(8,128)S(1)}, f32[16,2304]{1,0:T(8,128)S(1)}, u32[]{:S(2)}, u32[]{:S(2)}) collective-permute-start(f32[16,2304]{1,0:T(8,128)S(1)} %get-tuple-element.170), channel_id=1, source_target_pairs={{0,21},{1,22},{2,23},{3,24},{4,25},{5,26},{6,27},{7,28},{8,29},{9,... | collective-permute-start | bytes 442376
  922.1 14.6 %collective-permute-start.20 = (f32[16,2304]{1,0:T(8,128)S(1)}, f32[16,2304]{1,0:T(8,128)S(1)}, u32[]{:S(2)}, u32[]{:S(2)}) collective-permute-start(f32[16,2304]{1,0:T(8,128)S(1)} %get-tuple-element.170), channel_id=1, source_target_pairs={{0,19},{1,20},{2,21},{3,22},{4,23},{5,24},{6,25},{7,26},{8,27},{9,... | collective-permute-start | bytes 442376
  930.5 18.0 %collective-permute-start.17 = (f32[16,2304]{1,0:T(8,128)S(1)}, f32[16,2304]{1,0:T(8,128)S(1)}, u32[]{:S(2)}, u32[]{:S(2)}) collective-permute-start(f32[16,2304]{1,0:T(8,128)S(1)} %get-tuple-element.170), channel_id=1, source_target_pairs={{0,16},{1,17},{2,18},{3,19},{4,20},{5,21},{6,22},{7,23},{8,24},{9,... | collective-permute-start | bytes 442376
  932.4 17.4 %collective-permute-start.16 = (f32[16,2304]{1,0:T(8,128)S(1)}, f32[16,2304]{1,0:T(8,128)S(1)}, u32[]{:S(2)}, u32[]{:S(2)}) collective-permute-start(f32[16,2304]{1,0:T(8,128)S(1)} %get-tuple-element.170), channel_id=1, source_target_pairs={{0,15},{1,16},{2,17},{3,18},{4,19},{5,20},{6,21},{7,22},{8,23},{9,... | collective-permute-start | bytes 442376
  936.7 22.2 %collective-permute-start.15 = (f32[16,2304]{1,0:T(8,128)S(1)}, f32[16,2304]{1,0:T(8,128)S(1)}, u32[]{:S(2)}, u32[]{:S(2)}) collective-permute-start(f32[16,2304]{1,0:T(8,128)S(1)} %get-tuple-element.170), channel_id=1, source_target_pairs={{0,14},{1,15},{2,16},{3,17},{4,18},{5,19},{6,20},{7,21},{8,22},{9,... | collective-permute-start | bytes 442376
  938.4 22.5 %collective-permute-start.14 = (f32[16,2304]{1,0:T(8,128)S(1)}, f32[16,2304]{1,0:T(8,128)S(1)}, u32[]{:S(2)}, u32[]{:S(2)}) collective-permute-start(f32[16,2304]{1,0:T(8,128)S(1)} %get-tuple-element.170), channel_id=1, source_target_pairs={{0,13},{1,14},{2,15},{3,16},{4,17},{5,18},{6,19},{7,20},{8,21},{9,... | collective-permute-start | bytes 442376
  942.8 24.0 %collective-permute-start.13 = (f32[16,2304]{1,0:T(8,128)S(1)}, f32[16,2304]{1,0:T(8,128)S(1)}, u32[]{:S(2)}, u32[]{:S(2)}) collective-permute-start(f32[16,2304]{1,0:T(8,128)S(1)} %get-tuple-element.170), channel_id=1, source_target_pairs={{0,12},{1,13},{2,14},{3,15},{4,16},{5,17},{6,18},{7,19},{8,20},{9,... | collective-permute-start | bytes 442376
  948.5 20.5 %collective-permute-start.12 = (f32[16,2304]{1,0:T(8,128)S(1)}, f32[16,2304]{1,0:T(8,128)S(1)}, u32[]{:S(2)}, u32[]{:S(2)}) collective-permute-start(f32[16,2304]{1,0:T(8,128)S(1)} %get-tuple-element.170), channel_id=1, source_target_pairs={{0,11},{1,12},{2,13},{3,14},{4,15},{5,16},{6,17},{7,18},{8,19},{9,... | collective-permute-start | bytes 442376
  949.9 52.0 %collective-permute-start.11 = (f32[16,2304]{1,0:T(8,128)S(1)}, f32[16,2304]{1,0:T(8,128)}, u32[]{:S(2)}, u32[]{:S(2)}) collective-permute-start(f32[16,2304]{1,0:T(8,128)S(1)} %get-tuple-element.170), channel_id=1, source_target_pairs={{0,10},{1,11},{2,12},{3,13},{4,14},{5,15},{6,16},{7,17},{8,18},{9,... | collective-permute-start | bytes 442376
  959.0 52.9 %collective-permute-start.10 = (f32[16,2304]{1,0:T(8,128)S(1)}, f32[16,2304]{1,0:T(8,128)}, u32[]{:S(2)}, u32[]{:S(2)}) collective-permute-start(f32[16,2304]{1,0:T(8,128)S(1)} %get-tuple-element.170), channel_id=1, source_target_pairs={{0,9},{1,10},{2,11},{3,12},{4,13},{5,14},{6,15},{7,16},{8,17},{9,1... | collective-permute-start | bytes 442376
  960.9 53.1 %collective-permute-start.9 = (f32[16,2304]{1,0:T(8,128)S(1)}, f32[16,2304]{1,0:T(8,128)}, u32[]{:S(2)}, u32[]{:S(2)}) collective-permute-start(f32[16,2304]{1,0:T(8,128)S(1)} %get-tuple-element.170), channel_id=1, source_target_pairs={{0,8},{1,9},{2,10},{3,11},{4,12},{5,13},{6,14},{7,15},{8,16},{9,17... | collective-permute-start | bytes 442376
  966.8 49.8 %collective-permute-start.8 = (f32[16,2304]{1,0:T(8,128)S(1)}, f32[16,2304]{1,0:T(8,128)}, u32[]{:S(2)}, u32[]{:S(2)}) collective-permute-start(f32[16,2304]{1,0:T(8,128)S(1)} %get-tuple-element.170), channel_id=1, source_target_pairs={{0,7},{1,8},{2,9},{3,10},{4,11},{5,12},{6,13},{7,14},{8,15},{9,16}... | collective-permute-start | bytes 442376
  969.1 53.9 %collective-permute-start.7 = (f32[16,2304]{1,0:T(8,128)S(1)}, f32[16,2304]{1,0:T(8,128)}, u32[]{:S(2)}, u32[]{:S(2)}) collective-permute-start(f32[16,2304]{1,0:T(8,128)S(1)} %get-tuple-element.170), channel_id=1, source_target_pairs={{0,6},{1,7},{2,8},{3,9},{4,10},{5,11},{6,12},{7,13},{8,14},{9,15},... | collective-permute-start | bytes 442376
  1001.9 23.6 %collective-permute-start.6 = (f32[16,2304]{1,0:T(8,128)S(1)}, f32[16,2304]{1,0:T(8,128)S(1)}, u32[]{:S(2)}, u32[]{:S(2)}) collective-permute-start(f32[16,2304]{1,0:T(8,128)S(1)} %get-tuple-element.170), channel_id=1, source_target_pairs={{0,5},{1,6},{2,7},{3,8},{4,9},{5,10},{6,11},{7,12},{8,13},{9,14},{... | collective-permute-start | bytes 442376
  1011.9 13.7 %collective-permute-start.5 = (f32[16,2304]{1,0:T(8,128)S(1)}, f32[16,2304]{1,0:T(8,128)S(1)}, u32[]{:S(2)}, u32[]{:S(2)}) collective-permute-start(f32[16,2304]{1,0:T(8,128)S(1)} %get-tuple-element.170), channel_id=1, source_target_pairs={{0,4},{1,5},{2,6},{3,7},{4,8},{5,9},{6,10},{7,11},{8,12},{9,13},{1... | collective-permute-start | bytes 442376
  1014.1 14.3 %collective-permute-start.4 = (f32[16,2304]{1,0:T(8,128)S(1)}, f32[16,2304]{1,0:T(8,128)S(1)}, u32[]{:S(2)}, u32[]{:S(2)}) collective-permute-start(f32[16,2304]{1,0:T(8,128)S(1)} %get-tuple-element.170), channel_id=1, source_target_pairs={{0,3},{1,4},{2,5},{3,6},{4,7},{5,8},{6,9},{7,10},{8,11},{9,12},{10... | collective-permute-start | bytes 442376
  (99 other events, 2466.0 us)
Sparse Core Ops, SparseCore 0:
  9.7 146.3 all-gather.2
  157.7 64.8 all-gather.4
where the time goes:
time: 1110 us; the launch traced here: 1100 us
  blocking collectives  379 us (34%)
  waiting for transfers between devices  226 us (20%)
  starting transfers between devices  198 us (18%)
  local copies, waits for them, and re-layouts  167 us (15%)
  matrix products  93.3 us (8%)
  other arithmetic  16.8 us (2%)
  between operations  16.3 us (1%)
    unnamed x1, blocking collectives  379 us
    unnamed x64, starting transfers between devices  191 us
    all_gather x1, waiting for transfers between devices, body(): lax.all_gather(w_qkv, 'dp', axis=0, tiled=True)  145 us
    unnamed x164, local copies, waits for them, and re-layouts  95.8 us
    dot_general x5, matrix products, contract(): return jnp.einsum(form, left, right, preferred_element_type=jnp.float32)  60.5 us
    all_gather x1, waiting for transfers between devices, body(): lax.all_gather(w_out, 'dp', axis=0, tiled=True)  58 us
    unnamed x66, waiting for transfers between devices  23.2 us
    slice x20, local copies, waits for them, and re-layouts, windows(): blocked[shift_by:shift_by + stretch_count]  22.7 us
  transfers between devices with their start and end apart: 68, of which 8 were waited for; matrix products, arithmetic and copies ran while one was open for 9% of the time, Pallas kernels for 0%

commit v1 on v0

--- a/solution.py
+++ b/solution.py
@@ -8,6 +8,13 @@
 STRETCH = 64
 PRIOR = 4
 EPS = 1e-05
+
+
+def stacks_all_load(xs):
+    buffer = []
+    for _ in range(lax.axis_size("dp")):
+        buffer.append(xs)
+    return jnp.concatenate(lax.all_to_all(jnp.stack(buffer, axis=0), "dp", 0, 0), axis=0)
 
 
 def from_behind(value, axis, by):
@@ -120,10 +127,7 @@
     offset = lax.axis_index("seq") * frame_count
     normed, inv_sigma = normalize(own_frames)
     normed_low = normed.astype(jnp.bfloat16)
-    full_qkv, full_out = (
-        lax.all_gather(w_qkv, "dp", axis=0, tiled=True),
-        lax.all_gather(w_out, "dp", axis=0, tiled=True),
-    )
+    full_qkv, full_out = (stacks_all_load(w_qkv), lax.all_gather(w_out, "dp", axis=0, tiled=True))
     projected = jnp.dot(normed_low, full_qkv, preferred_element_type=jnp.float32)
     projected = projected.astype(jnp.bfloat16)
     queries = projected[:, :inner_width]

time: 1110 us -> 1050 us (0.946)
  waiting for transfers between devices: 226 us -> 148 us
  blocking collectives: 379 us -> 391 us
    all_gather x1 -> x0, waiting for transfers between devices: 145 us -> none  [body(): lax.all_gather(w_qkv, 'dp', axis=0, tiled=True)]
    all_to_all x0 -> x1, waiting for transfers between devices: none -> 123 us  [stacks_all_load(): lax.all_to_all(jnp.stack(buffer, axis=0), 'dp', 0, 0)]
    all_gather x1, waiting for transfers between devices: 58 us -> 0.02 us  [body(): lax.all_gather(w_out, 'dp', axis=0, tiled=True)]
    unnamed x1, blocking collectives: 379 us -> 391 us
    unnamed x66 -> x65, waiting for transfers between devices: 23.2 us -> 22.5 us
    unnamed x164 -> x166, local copies, waits for them, and re-layouts: 95.8 us -> 95.8 us
where the time goes in v1:
time: 1050 us; the launch traced here: 1040 us
  blocking collectives  391 us (37%)
  starting transfers between devices  205 us (20%)
  local copies, waits for them, and re-layouts  171 us (16%)
  waiting for transfers between devices  148 us (14%)
  matrix products  93.3 us (9%)
  between operations  16.4 us (2%)
  other arithmetic  15.7 us (1%)
    unnamed x1, blocking collectives  391 us
    unnamed x64, starting transfers between devices  192 us
    all_to_all x1, waiting for transfers between devices, stacks_all_load(): lax.all_to_all(jnp.stack(buffer, axis=0), 'dp', 0, 0)  123 us
    unnamed x166, local copies, waits for them, and re-layouts  95.8 us
    dot_general x5, matrix products, contract(): return jnp.einsum(form, left, right, preferred_element_type=jnp.float32)  60.5 us
    slice x20, local copies, waits for them, and re-layouts, windows(): blocked[shift_by:shift_by + stretch_count]  22.7 us
    unnamed x65, waiting for transfers between devices  22.5 us
  transfers between devices with their start and end apart: 68, of which 8 were waited for; matrix products, arithmetic and copies ran while one was open for 9% of the time, Pallas kernels for 0%

profile of v1, /device:TPU:8, one launch (start us, length us, event | category | flops | bytes accessed | tf_op | source)
XLA Modules:
  0.0 1040.2 jit_solution(12390899254085569163)
XLA Ops:
  7.2 4.6 stack.32
  11.8 6.4 all-to-all-start
  19.5 123.3 %all-to-all-done = bf16[8,192,2304]{2,1,0:T(8,128)(2,1)} async-done(((bf16[8,192,2304]{2,1,0:T(8,128)(2,1)}), bf16[8,192,2304]{2,1,0:T(8,128)(2,1)}, u32[]{:S(2)}, u32[]{:S(2)}) %all-to-all-start) | async-done | bytes 7077920 | tf_op jit(solution)/shard_map/all_to_all | solution.py:17
  142.8 5.1 convolution_convert_fusion
  188.0 4.6 concatenate.42
  192.6 4.2 fusion.94
  196.8 5.8 concatenate.44
  202.6 6.3 fusion.93
  208.9 4.4 fusion.53
  213.3 2.8 convolution_bitcast_fusion
  216.1 6.9 copy.108
  229.7 24.8 %fusion.20 = f32[4,320,12,64]{1,3,2,0:T(8,128)} fusion(bf16[4,64,12,64]{1,3,2,0:T(8,128)(2,1)S(1)} %copy-done.19, f32[4,12,64,320]{3,2,1,0:T(8,128)} %fusion.94, f32[4,12,64,320]{3,2,1,0:T(8,128)} %get-tuple-element.190, f32[4,12,64]{2,1,0:T(8,128)S(1)} %get-tuple-element.189), kind=kOutput, calls=%fused_computation.23 | convolution fusion | flops 132713792 | bytes 12201984 | tf_op jit(solution)/shard_map/nhqk,nqhd->nkhd/dot_general | solution.py:34
  255.6 6.9 copy.100
  271.9 4.2 collective-permute-start.1
  276.1 24.3 %fusion.54 = bf16[4,64,12,64]{1,3,2,0:T(8,128)(2,1)S(1)} fusion(bf16[4,320,12,64]{1,3,2,0:T(8,128)(2,1)} %concatenate.44, f32[4,12,64,320]{3,2,1,0:T(8,128)} %fusion.94, f32[4,12,64,320]{3,2,1,0:T(8,128)} %get-tuple-element.190, f32[4,12,64]{2,1,0:T(8,128)} %copy-done.79), kind=kOutput, calls=%fused_computation.66 | convolution fusion | flops 132910400 | bytes 10235904 | tf_op jit(solution)/shard_map/nhqk,nkhd->nqhd/dot_general | solution.py:34
  306.4 3.4 fusion.43
  313.4 3.0 fusion.68
  319.1 7.3 fusion.60
  326.4 391.4 %fusion.91 = (f32[16,2304]{1,0:T(8,128)S(1)}, f32[8,1536]{1,0:T(8,128)S(1)}) fusion(f32[1536,2304]{1,0:T(8,128)} %fusion.60, f32[768,1536]{1,0:T(8,128)} %fusion.68), kind=kCustom, calls=%all-reduce-scatter.2 | all-reduce-scatter fusion | flops 6291458 | bytes 19070976
  721.9 12.4 %collective-permute-start.62 = (f32[8,1536]{1,0:T(8,128)S(1)}, f32[8,1536]{1,0:T(8,128)S(1)}, u32[]{:S(2)}, u32[]{:S(2)}) collective-permute-start(f32[8,1536]{1,0:T(8,128)S(1)} %get-tuple-element.171), channel_id=1, source_target_pairs={{0,29},{1,30},{2,31},{3,32},{4,33},{5,34},{6,35},{7,36},{8,37},{9,... | collective-permute-start | bytes 147464
  742.5 15.7 %collective-permute-start.55 = (f32[8,1536]{1,0:T(8,128)S(1)}, f32[8,1536]{1,0:T(8,128)S(1)}, u32[]{:S(2)}, u32[]{:S(2)}) collective-permute-start(f32[8,1536]{1,0:T(8,128)S(1)} %get-tuple-element.171), channel_id=1, source_target_pairs={{0,22},{1,23},{2,24},{3,25},{4,26},{5,27},{6,28},{7,29},{8,30},{9,... | collective-permute-start | bytes 147464
  759.5 2.6 collective-permute-start.53
  762.1 2.9 collective-permute-start.52
  769.9 3.1 collective-permute-start.48
  775.5 3.5 collective-permute-start.46
  783.7 5.1 collective-permute-start.43
  792.5 5.8 collective-permute-start.40
  802.8 2.5 collective-permute-start.39
  807.3 2.8 collective-permute-start.37
  810.1 6.1 collective-permute-start.36
  816.2 3.1 collective-permute-start.35
  830.0 3.1 collective-permute-start.27
  833.1 3.3 fusion.14
  841.1 11.2 %collective-permute-done.29 = f32[16,2304]{1,0:T(8,128)S(1)} collective-permute-done((f32[16,2304]{1,0:T(8,128)S(1)}, f32[16,2304]{1,0:T(8,128)S(1)}, u32[]{:S(2)}, u32[]{:S(2)}) %collective-permute-start.29) | collective-permute-done | bytes 147488
  853.6 3.2 collective-permute-start.23
  859.0 5.3 fusion.90
  865.7 4.6 collective-permute-start.20
  876.0 4.3 collective-permute-start.16
  882.0 4.3 collective-permute-start.14
  886.3 5.7 collective-permute-start.13
  893.4 9.1 collective-permute-start.11
  904.5 5.9 collective-permute-start.9
  916.6 28.8 %concatenate.47 = f32[262,1536]{1,0:T(8,128)S(1)} concatenate(f32[6,1536]{1,0:T(8,128)} %copy-done.49, f32[8,1536]{1,0:T(8,128)S(1)} %collective-permute-done.64, f32[8,1536]{1,0:T(8,128)} %copy-done.50, f32[8,1536]{1,0:T(8,128)} %copy-done.51, f32[8,1536]{1,0:T(8,128)} %copy-done.52, f32[8,1536]{1,0:T(8,128)} %copy-done.53, f32[8,1536]{1,0:T(8,128)} %copy-done.54, ...), dimensions={0} | concatenate | bytes 3219456
  945.5 10.0 collective-permute-start.6
  957.7 2.5 collective-permute-start.4
  960.2 6.3 collective-permute-start.3
  969.1 2.8 collective-permute-done.4
  975.6 56.0 %concatenate.46 = f32[524,2304]{1,0:T(8,128)} concatenate(f32[12,2304]{1,0:T(8,128)} %collective-permute-done.33, f32[16,2304]{1,0:T(8,128)} %collective-permute-done.32, f32[16,2304]{1,0:T(8,128)S(1)} %copy-done.22, f32[16,2304]{1,0:T(8,128)S(1)} %copy-done.24, f32[16,2304]{1,0:T(8,128)S(1)} %copy-done.26, f32[16,2304]{1,0:T(8,128)S(1)} %collective-permute-done.28, ...), dimensions={0} | concatenate | bytes 9658368
  (343 shorter events, 152.2 us)
Async XLA Ops:
  11.8 131.0 %all-to-all-start = ((bf16[8,192,2304]{2,1,0:T(8,128)(2,1)}), bf16[8,192,2304]{2,1,0:T(8,128)(2,1)}, u32[]{:S(2)}, u32[]{:S(2)}) async-start(bf16[8,192,2304]{2,1,0:T(8,128)(2,1)} %stack.32), calls=%async_computation | async-start | bytes 14155776 | tf_op jit(solution)/shard_map/all_to_all | solution.py:17
  18.1 133.2 %all-gather.2.cloned.1.call-start = ((), (), s32[]{:S(2)}) async-start(), calls=%async_computation.1 | async-start | bytes 2654208 | tf_op jit(solution)/shard_map/all_gather | solution.py:130
  149.0 16.0 %collective-permute-start = (bf16[2,256,768]{2,1,0:T(8,128)(2,1)}, bf16[2,256,768]{2,1,0:T(8,128)(2,1)}, u32[]{:S(2)}, u32[]{:S(2)}) collective-permute-start(bf16[2,256,768]{2,1,0:T(8,128)(2,1)} %pad_maximum_fusion.1), channel_id=1, source_target_pairs={{0,1},{1,2},{2,3},{3,4},{4,5},{5,6},{6,7},{7,8},{8,9},{9,10},{10,1... | collective-permute-start | bytes 2359304 | tf_op jit(solution)/shard_map/ppermute | solution.py:23
  271.9 44.5 %collective-permute-start.1 = (bf16[2,256,768]{1,2,0:T(8,128)(2,1)}, bf16[2,256,768]{1,2,0:T(8,128)(2,1)}, u32[]{:S(2)}, u32[]{:S(2)}) collective-permute-start(bf16[2,256,768]{1,2,0:T(8,128)(2,1)} %pad_maximum_fusion.2), channel_id=1, source_target_pairs={{1,0},{2,1},{3,2},{4,3},{5,4},{6,5},{7,6},{8,7},{9,8},{10,9},{11,1... | collective-permute-start | bytes 2359304 | tf_op jit(solution)/shard_map/ppermute | solution.py:23
  717.9 19.3 %collective-permute-start.64 = (f32[8,1536]{1,0:T(8,128)S(1)}, f32[8,1536]{1,0:T(8,128)S(1)}, u32[]{:S(2)}, u32[]{:S(2)}) collective-permute-start(f32[8,1536]{1,0:T(8,128)S(1)} %get-tuple-element.171), channel_id=1, source_target_pairs={{0,31},{1,32},{2,33},{3,34},{4,35},{5,36},{6,37},{7,38},{8,39},{9,... | collective-permute-start | bytes 147464
  719.3 16.6 %collective-permute-start.65 = (f32[6,1536]{1,0:T(8,128)S(1)}, f32[6,1536]{1,0:T(8,128)S(1)}, u32[]{:S(2)}, u32[]{:S(2)}) collective-permute-start(f32[6,1536]{1,0:T(8,128)S(1)} %slice.520), channel_id=1, source_target_pairs={{0,32},{1,33},{2,34},{3,35},{4,36},{5,37},{6,38},{7,39},{8,40},{9,... | collective-permute-start | bytes 110600
  720.6 17.9 %collective-permute-start.63 = (f32[8,1536]{1,0:T(8,128)S(1)}, f32[8,1536]{1,0:T(8,128)S(1)}, u32[]{:S(2)}, u32[]{:S(2)}) collective-permute-start(f32[8,1536]{1,0:T(8,128)S(1)} %get-tuple-element.171), channel_id=1, source_target_pairs={{0,30},{1,31},{2,32},{3,33},{4,34},{5,35},{6,36},{7,37},{8,38},{9,... | collective-permute-start | bytes 147464
  721.9 17.9 %collective-permute-start.62 = (f32[8,1536]{1,0:T(8,128)S(1)}, f32[8,1536]{1,0:T(8,128)S(1)}, u32[]{:S(2)}, u32[]{:S(2)}) collective-permute-start(f32[8,1536]{1,0:T(8,128)S(1)} %get-tuple-element.171), channel_id=1, source_target_pairs={{0,29},{1,30},{2,31},{3,32},{4,33},{5,34},{6,35},{7,36},{8,37},{9,... | collective-permute-start | bytes 147464
  737.2 21.0 %collective-permute-start.59 = (f32[8,1536]{1,0:T(8,128)S(1)}, f32[8,1536]{1,0:T(8,128)S(1)}, u32[]{:S(2)}, u32[]{:S(2)}) collective-permute-start(f32[8,1536]{1,0:T(8,128)S(1)} %get-tuple-element.171), channel_id=1, source_target_pairs={{0,26},{1,27},{2,28},{3,29},{4,30},{5,31},{6,32},{7,33},{8,34},{9,... | collective-permute-start | bytes 147464
  738.6 21.0 %collective-permute-start.58 = (f32[8,1536]{1,0:T(8,128)S(1)}, f32[8,1536]{1,0:T(8,128)S(1)}, u32[]{:S(2)}, u32[]{:S(2)}) collective-permute-start(f32[8,1536]{1,0:T(8,128)S(1)} %get-tuple-element.171), channel_id=1, source_target_pairs={{0,25},{1,26},{2,27},{3,28},{4,29},{5,30},{6,31},{7,32},{8,33},{9,... | collective-permute-start | bytes 147464
  739.9 22.2 %collective-permute-start.57 = (f32[8,1536]{1,0:T(8,128)S(1)}, f32[8,1536]{1,0:T(8,128)S(1)}, u32[]{:S(2)}, u32[]{:S(2)}) collective-permute-start(f32[8,1536]{1,0:T(8,128)S(1)} %get-tuple-element.171), channel_id=1, source_target_pairs={{0,24},{1,25},{2,26},{3,27},{4,28},{5,29},{6,30},{7,31},{8,32},{9,... | collective-permute-start | bytes 147464
  741.2 23.8 %collective-permute-start.56 = (f32[8,1536]{1,0:T(8,128)S(1)}, f32[8,1536]{1,0:T(8,128)S(1)}, u32[]{:S(2)}, u32[]{:S(2)}) collective-permute-start(f32[8,1536]{1,0:T(8,128)S(1)} %get-tuple-element.171), channel_id=1, source_target_pairs={{0,23},{1,24},{2,25},{3,26},{4,27},{5,28},{6,29},{7,30},{8,31},{9,... | collective-permute-start | bytes 147464
  742.5 24.7 %collective-permute-start.55 = (f32[8,1536]{1,0:T(8,128)S(1)}, f32[8,1536]{1,0:T(8,128)S(1)}, u32[]{:S(2)}, u32[]{:S(2)}) collective-permute-start(f32[8,1536]{1,0:T(8,128)S(1)} %get-tuple-element.171), channel_id=1, source_target_pairs={{0,22},{1,23},{2,24},{3,25},{4,26},{5,27},{6,28},{7,29},{8,30},{9,... | collective-permute-start | bytes 147464
  769.9 13.8 %collective-permute-start.48 = (f32[8,1536]{1,0:T(8,128)S(1)}, f32[8,1536]{1,0:T(8,128)S(1)}, u32[]{:S(2)}, u32[]{:S(2)}) collective-permute-start(f32[8,1536]{1,0:T(8,128)S(1)} %get-tuple-element.171), channel_id=1, source_target_pairs={{0,15},{1,16},{2,17},{3,18},{4,19},{5,20},{6,21},{7,22},{8,23},{9,... | collective-permute-start | bytes 147464
  773.0 15.8 %collective-permute-start.47 = (f32[8,1536]{1,0:T(8,128)S(1)}, f32[8,1536]{1,0:T(8,128)S(1)}, u32[]{:S(2)}, u32[]{:S(2)}) collective-permute-start(f32[8,1536]{1,0:T(8,128)S(1)} %get-tuple-element.171), channel_id=1, source_target_pairs={{0,14},{1,15},{2,16},{3,17},{4,18},{5,19},{6,20},{7,21},{8,22},{9,... | collective-permute-start | bytes 147464
  775.5 14.7 %collective-permute-start.46 = (f32[8,1536]{1,0:T(8,128)S(1)}, f32[8,1536]{1,0:T(8,128)S(1)}, u32[]{:S(2)}, u32[]{:S(2)}) collective-permute-start(f32[8,1536]{1,0:T(8,128)S(1)} %get-tuple-element.171), channel_id=1, source_target_pairs={{0,13},{1,14},{2,15},{3,16},{4,17},{5,18},{6,19},{7,20},{8,21},{9,... | collective-permute-start | bytes 147464
  781.2 17.0 %collective-permute-start.44 = (f32[8,1536]{1,0:T(8,128)S(1)}, f32[8,1536]{1,0:T(8,128)S(1)}, u32[]{:S(2)}, u32[]{:S(2)}) collective-permute-start(f32[8,1536]{1,0:T(8,128)S(1)} %get-tuple-element.171), channel_id=1, source_target_pairs={{0,11},{1,12},{2,13},{3,14},{4,15},{5,16},{6,17},{7,18},{8,19},{9,... | collective-permute-start | bytes 147464
  783.7 17.1 %collective-permute-start.43 = (f32[8,1536]{1,0:T(8,128)S(1)}, f32[8,1536]{1,0:T(8,128)S(1)}, u32[]{:S(2)}, u32[]{:S(2)}) collective-permute-start(f32[8,1536]{1,0:T(8,128)S(1)} %get-tuple-element.171), channel_id=1, source_target_pairs={{0,10},{1,11},{2,12},{3,13},{4,14},{5,15},{6,16},{7,17},{8,18},{9,... | collective-permute-start | bytes 147464
  788.9 13.9 %collective-permute-start.42 = (f32[8,1536]{1,0:T(8,128)S(1)}, f32[8,1536]{1,0:T(8,128)S(1)}, u32[]{:S(2)}, u32[]{:S(2)}) collective-permute-start(f32[8,1536]{1,0:T(8,128)S(1)} %get-tuple-element.171), channel_id=1, source_target_pairs={{0,9},{1,10},{2,11},{3,12},{4,13},{5,14},{6,15},{7,16},{8,17},{9,1... | collective-permute-start | bytes 147464
  790.2 15.2 %collective-permute-start.41 = (f32[8,1536]{1,0:T(8,128)S(1)}, f32[8,1536]{1,0:T(8,128)S(1)}, u32[]{:S(2)}, u32[]{:S(2)}) collective-permute-start(f32[8,1536]{1,0:T(8,128)S(1)} %get-tuple-element.171), channel_id=1, source_target_pairs={{0,8},{1,9},{2,10},{3,11},{4,12},{5,13},{6,14},{7,15},{8,16},{9,17... | collective-permute-start | bytes 147464
  792.5 14.8 %collective-permute-start.40 = (f32[8,1536]{1,0:T(8,128)S(1)}, f32[8,1536]{1,0:T(8,128)S(1)}, u32[]{:S(2)}, u32[]{:S(2)}) collective-permute-start(f32[8,1536]{1,0:T(8,128)S(1)} %get-tuple-element.171), channel_id=1, source_target_pairs={{0,7},{1,8},{2,9},{3,10},{4,11},{5,12},{6,13},{7,14},{8,15},{9,16}... | collective-permute-start | bytes 147464
  798.9 31.1 %collective-permute-start.32 = (f32[16,2304]{1,0:T(8,128)S(1)}, f32[16,2304]{1,0:T(8,128)}, u32[]{:S(2)}, u32[]{:S(2)}) collective-permute-start(f32[16,2304]{1,0:T(8,128)S(1)} %get-tuple-element.170), channel_id=1, source_target_pairs={{0,31},{1,32},{2,33},{3,34},{4,35},{5,36},{6,37},{7,38},{8,39},{9,... | collective-permute-start | bytes 442376
  800.9 27.7 %collective-permute-start.33 = (f32[12,2304]{1,0:T(8,128)S(1)}, f32[12,2304]{1,0:T(8,128)}, u32[]{:S(2)}, u32[]{:S(2)}) collective-permute-start(f32[12,2304]{1,0:T(8,128)S(1)} %slice.519), channel_id=1, source_target_pairs={{0,32},{1,33},{2,34},{3,35},{4,36},{5,37},{6,38},{7,39},{8,40},{9,... | collective-permute-start | bytes 331784
  821.4 15.0 %collective-permute-start.31 = (f32[16,2304]{1,0:T(8,128)S(1)}, f32[16,2304]{1,0:T(8,128)S(1)}, u32[]{:S(2)}, u32[]{:S(2)}) collective-permute-start(f32[16,2304]{1,0:T(8,128)S(1)} %get-tuple-element.170), channel_id=1, source_target_pairs={{0,30},{1,31},{2,32},{3,33},{4,34},{5,35},{6,36},{7,37},{8,38},{9,... | collective-permute-start | bytes 442376
  824.7 15.1 %collective-permute-start.30 = (f32[16,2304]{1,0:T(8,128)S(1)}, f32[16,2304]{1,0:T(8,128)S(1)}, u32[]{:S(2)}, u32[]{:S(2)}) collective-permute-start(f32[16,2304]{1,0:T(8,128)S(1)} %get-tuple-element.170), channel_id=1, source_target_pairs={{0,29},{1,30},{2,31},{3,32},{4,33},{5,34},{6,35},{7,36},{8,37},{9,... | collective-permute-start | bytes 442376
  827.3 25.0 %collective-permute-start.29 = (f32[16,2304]{1,0:T(8,128)S(1)}, f32[16,2304]{1,0:T(8,128)S(1)}, u32[]{:S(2)}, u32[]{:S(2)}) collective-permute-start(f32[16,2304]{1,0:T(8,128)S(1)} %get-tuple-element.170), channel_id=1, source_target_pairs={{0,28},{1,29},{2,30},{3,31},{4,32},{5,33},{6,34},{7,35},{8,36},{9,... | collective-permute-start | bytes 442376
  828.6 25.0 %collective-permute-start.28 = (f32[16,2304]{1,0:T(8,128)S(1)}, f32[16,2304]{1,0:T(8,128)S(1)}, u32[]{:S(2)}, u32[]{:S(2)}) collective-permute-start(f32[16,2304]{1,0:T(8,128)S(1)} %get-tuple-element.170), channel_id=1, source_target_pairs={{0,27},{1,28},{2,29},{3,30},{4,31},{5,32},{6,33},{7,34},{8,35},{9,... | collective-permute-start | bytes 442376
  830.0 26.9 %collective-permute-start.27 = (f32[16,2304]{1,0:T(8,128)S(1)}, f32[16,2304]{1,0:T(8,128)S(1)}, u32[]{:S(2)}, u32[]{:S(2)}) collective-permute-start(f32[16,2304]{1,0:T(8,128)S(1)} %get-tuple-element.170), channel_id=1, source_target_pairs={{0,26},{1,27},{2,28},{3,29},{4,30},{5,31},{6,32},{7,33},{8,34},{9,... | collective-permute-start | bytes 442376
  836.4 27.9 %collective-permute-start.26 = (f32[16,2304]{1,0:T(8,128)S(1)}, f32[16,2304]{1,0:T(8,128)S(1)}, u32[]{:S(2)}, u32[]{:S(2)}) collective-permute-start(f32[16,2304]{1,0:T(8,128)S(1)} %get-tuple-element.170), channel_id=1, source_target_pairs={{0,25},{1,26},{2,27},{3,28},{4,29},{5,30},{6,31},{7,32},{8,33},{9,... | collective-permute-start | bytes 442376
  839.8 25.8 %collective-permute-start.25 = (f32[16,2304]{1,0:T(8,128)S(1)}, f32[16,2304]{1,0:T(8,128)S(1)}, u32[]{:S(2)}, u32[]{:S(2)}) collective-permute-start(f32[16,2304]{1,0:T(8,128)S(1)} %get-tuple-element.170), channel_id=1, source_target_pairs={{0,24},{1,25},{2,26},{3,27},{4,28},{5,29},{6,30},{7,31},{8,32},{9,... | collective-permute-start | bytes 442376
  852.3 17.9 %collective-permute-start.24 = (f32[16,2304]{1,0:T(8,128)S(1)}, f32[16,2304]{1,0:T(8,128)S(1)}, u32[]{:S(2)}, u32[]{:S(2)}) collective-permute-start(f32[16,2304]{1,0:T(8,128)S(1)} %get-tuple-element.170), channel_id=1, source_target_pairs={{0,23},{1,24},{2,25},{3,26},{4,27},{5,28},{6,29},{7,30},{8,31},{9,... | collective-permute-start | bytes 442376
  853.6 19.1 %collective-permute-start.23 = (f32[16,2304]{1,0:T(8,128)S(1)}, f32[16,2304]{1,0:T(8,128)S(1)}, u32[]{:S(2)}, u32[]{:S(2)}) collective-permute-start(f32[16,2304]{1,0:T(8,128)S(1)} %get-tuple-element.170), channel_id=1, source_target_pairs={{0,22},{1,23},{2,24},{3,25},{4,26},{5,27},{6,28},{7,29},{8,30},{9,... | collective-permute-start | bytes 442376
  857.5 16.6 %collective-permute-start.22 = (f32[16,2304]{1,0:T(8,128)S(1)}, f32[16,2304]{1,0:T(8,128)S(1)}, u32[]{:S(2)}, u32[]{:S(2)}) collective-permute-start(f32[16,2304]{1,0:T(8,128)S(1)} %get-tuple-element.170), channel_id=1, source_target_pairs={{0,21},{1,22},{2,23},{3,24},{4,25},{5,26},{6,27},{7,28},{8,29},{9,... | collective-permute-start | bytes 442376
  865.7 14.6 %collective-permute-start.20 = (f32[16,2304]{1,0:T(8,128)S(1)}, f32[16,2304]{1,0:T(8,128)S(1)}, u32[]{:S(2)}, u32[]{:S(2)}) collective-permute-start(f32[16,2304]{1,0:T(8,128)S(1)} %get-tuple-element.170), channel_id=1, source_target_pairs={{0,19},{1,20},{2,21},{3,22},{4,23},{5,24},{6,25},{7,26},{8,27},{9,... | collective-permute-start | bytes 442376
  874.1 18.0 %collective-permute-start.17 = (f32[16,2304]{1,0:T(8,128)S(1)}, f32[16,2304]{1,0:T(8,128)S(1)}, u32[]{:S(2)}, u32[]{:S(2)}) collective-permute-start(f32[16,2304]{1,0:T(8,128)S(1)} %get-tuple-element.170), channel_id=1, source_target_pairs={{0,16},{1,17},{2,18},{3,19},{4,20},{5,21},{6,22},{7,23},{8,24},{9,... | collective-permute-start | bytes 442376
  876.0 17.4 %collective-permute-start.16 = (f32[16,2304]{1,0:T(8,128)S(1)}, f32[16,2304]{1,0:T(8,128)S(1)}, u32[]{:S(2)}, u32[]{:S(2)}) collective-permute-start(f32[16,2304]{1,0:T(8,128)S(1)} %get-tuple-element.170), channel_id=1, source_target_pairs={{0,15},{1,16},{2,17},{3,18},{4,19},{5,20},{6,21},{7,22},{8,23},{9,... | collective-permute-start | bytes 442376
  880.3 22.2 %collective-permute-start.15 = (f32[16,2304]{1,0:T(8,128)S(1)}, f32[16,2304]{1,0:T(8,128)S(1)}, u32[]{:S(2)}, u32[]{:S(2)}) collective-permute-start(f32[16,2304]{1,0:T(8,128)S(1)} %get-tuple-element.170), channel_id=1, source_target_pairs={{0,14},{1,15},{2,16},{3,17},{4,18},{5,19},{6,20},{7,21},{8,22},{9,... | collective-permute-start | bytes 442376
  882.0 22.4 %collective-permute-start.14 = (f32[16,2304]{1,0:T(8,128)S(1)}, f32[16,2304]{1,0:T(8,128)S(1)}, u32[]{:S(2)}, u32[]{:S(2)}) collective-permute-start(f32[16,2304]{1,0:T(8,128)S(1)} %get-tuple-element.170), channel_id=1, source_target_pairs={{0,13},{1,14},{2,15},{3,16},{4,17},{5,18},{6,19},{7,20},{8,21},{9,... | collective-permute-start | bytes 442376
  886.3 24.0 %collective-permute-start.13 = (f32[16,2304]{1,0:T(8,128)S(1)}, f32[16,2304]{1,0:T(8,128)S(1)}, u32[]{:S(2)}, u32[]{:S(2)}) collective-permute-start(f32[16,2304]{1,0:T(8,128)S(1)} %get-tuple-element.170), channel_id=1, source_target_pairs={{0,12},{1,13},{2,14},{3,15},{4,16},{5,17},{6,18},{7,19},{8,20},{9,... | collective-permute-start | bytes 442376
  892.1 20.5 %collective-permute-start.12 = (f32[16,2304]{1,0:T(8,128)S(1)}, f32[16,2304]{1,0:T(8,128)S(1)}, u32[]{:S(2)}, u32[]{:S(2)}) collective-permute-start(f32[16,2304]{1,0:T(8,128)S(1)} %get-tuple-element.170), channel_id=1, source_target_pairs={{0,11},{1,12},{2,13},{3,14},{4,15},{5,16},{6,17},{7,18},{8,19},{9,... | collective-permute-start | bytes 442376
  893.4 52.0 %collective-permute-start.11 = (f32[16,2304]{1,0:T(8,128)S(1)}, f32[16,2304]{1,0:T(8,128)}, u32[]{:S(2)}, u32[]{:S(2)}) collective-permute-start(f32[16,2304]{1,0:T(8,128)S(1)} %get-tuple-element.170), channel_id=1, source_target_pairs={{0,10},{1,11},{2,12},{3,13},{4,14},{5,15},{6,16},{7,17},{8,18},{9,... | collective-permute-start | bytes 442376
  902.5 52.9 %collective-permute-start.10 = (f32[16,2304]{1,0:T(8,128)S(1)}, f32[16,2304]{1,0:T(8,128)}, u32[]{:S(2)}, u32[]{:S(2)}) collective-permute-start(f32[16,2304]{1,0:T(8,128)S(1)} %get-tuple-element.170), channel_id=1, source_target_pairs={{0,9},{1,10},{2,11},{3,12},{4,13},{5,14},{6,15},{7,16},{8,17},{9,1... | collective-permute-start | bytes 442376
  904.5 53.2 %collective-permute-start.9 = (f32[16,2304]{1,0:T(8,128)S(1)}, f32[16,2304]{1,0:T(8,128)}, u32[]{:S(2)}, u32[]{:S(2)}) collective-permute-start(f32[16,2304]{1,0:T(8,128)S(1)} %get-tuple-element.170), channel_id=1, source_target_pairs={{0,8},{1,9},{2,10},{3,11},{4,12},{5,13},{6,14},{7,15},{8,16},{9,17... | collective-permute-start | bytes 442376
  910.3 49.9 %collective-permute-start.8 = (f32[16,2304]{1,0:T(8,128)S(1)}, f32[16,2304]{1,0:T(8,128)}, u32[]{:S(2)}, u32[]{:S(2)}) collective-permute-start(f32[16,2304]{1,0:T(8,128)S(1)} %get-tuple-element.170), channel_id=1, source_target_pairs={{0,7},{1,8},{2,9},{3,10},{4,11},{5,12},{6,13},{7,14},{8,15},{9,16}... | collective-permute-start | bytes 442376
  912.6 53.9 %collective-permute-start.7 = (f32[16,2304]{1,0:T(8,128)S(1)}, f32[16,2304]{1,0:T(8,128)}, u32[]{:S(2)}, u32[]{:S(2)}) collective-permute-start(f32[16,2304]{1,0:T(8,128)S(1)} %get-tuple-element.170), channel_id=1, source_target_pairs={{0,6},{1,7},{2,8},{3,9},{4,10},{5,11},{6,12},{7,13},{8,14},{9,15},... | collective-permute-start | bytes 442376
  945.5 23.7 %collective-permute-start.6 = (f32[16,2304]{1,0:T(8,128)S(1)}, f32[16,2304]{1,0:T(8,128)S(1)}, u32[]{:S(2)}, u32[]{:S(2)}) collective-permute-start(f32[16,2304]{1,0:T(8,128)S(1)} %get-tuple-element.170), channel_id=1, source_target_pairs={{0,5},{1,6},{2,7},{3,8},{4,9},{5,10},{6,11},{7,12},{8,13},{9,14},{... | collective-permute-start | bytes 442376
  955.5 13.7 %collective-permute-start.5 = (f32[16,2304]{1,0:T(8,128)S(1)}, f32[16,2304]{1,0:T(8,128)S(1)}, u32[]{:S(2)}, u32[]{:S(2)}) collective-permute-start(f32[16,2304]{1,0:T(8,128)S(1)} %get-tuple-element.170), channel_id=1, source_target_pairs={{0,4},{1,5},{2,6},{3,7},{4,8},{5,9},{6,10},{7,11},{8,12},{9,13},{1... | collective-permute-start | bytes 442376
  957.7 14.3 %collective-permute-start.4 = (f32[16,2304]{1,0:T(8,128)S(1)}, f32[16,2304]{1,0:T(8,128)S(1)}, u32[]{:S(2)}, u32[]{:S(2)}) collective-permute-start(f32[16,2304]{1,0:T(8,128)S(1)} %get-tuple-element.170), channel_id=1, source_target_pairs={{0,3},{1,4},{2,5},{3,6},{4,7},{5,8},{6,9},{7,10},{8,11},{9,12},{10... | collective-permute-start | bytes 442376
  (100 other events, 2408.9 us)
Sparse Core Ops, SparseCore 0:
  20.6 101.9 all-gather.1
